TPU v7x, 128 devices: a whole 4x4x4 slice. The times are simulated.
128 devices in a mesh: scen: 2 (over x_hi), hour: 16 (over z, y), reg: 4 (over x_lo, core).
Axes of the slice: x: 4 (x_hi: 2, x_lo: 2; x = x_hi * 2 + x_lo), y: 4, z: 4, core: 2. Of those that a mesh axis runs over, the one named last changes fastest.
Arguments:
- cost_rate: float32 [8, 2688, 2048], P('scen', 'hour', 'reg'), may hold values from 0.05 to 1
- invest_cost: float32 [3, 2048], P(None, 'reg'), may hold values from 0.1 to 1
- tile: bfloat16 [16, 256, 2048], P('hour', None, 'reg'), may hold values from -0.1875 to 0.1875
- tile_mask: int32 [16, 256, 2048], P('hour', None, 'reg'), may hold values 0 or 1
- demand: float32 [8, 2688, 256], P('scen', 'hour'), may hold values from -6 to 6
- dispatch: float32 [8, 2688, 2048], P('scen', 'hour', 'reg'), may hold values from 0 to 1
- dual: float32 [8, 2688, 256], P('scen', 'hour'), may hold values from 0 to 1
- cap_dual: float32 [8, 2688, 2048], P('scen', 'hour', 'reg'), may hold values from 0 to 1
- capacity: float32 [8, 3, 2048], P('scen', None, 'reg'), may hold values from 0 to 2
- multiplier: float32 [8, 3, 2048], P('scen', None, 'reg'), may hold values from -3 to 3
- consensus: float32 [8, 3, 2048], P('scen', None, 'reg'), may hold values from 0 to 2
- scen_weight: float32 [8], P('scen'), may hold values from 0.1 to 1
- node_of: int32 [3, 8], P(None, 'scen'), may hold values from 0 to 3, as said below
Outputs:
- dispatch_out: float32 [8, 2688, 2048], P('scen', 'hour', 'reg')
- dual_out: float32 [8, 2688, 256], P('scen', 'hour', 'reg')
- capacity_out: float32 [8, 3, 2048], P('scen', None, 'reg')
- multiplier_out: float32 [8, 3, 2048], P('scen', None, 'reg')
Inputs may be any that keep to these rules, and one draw needn't show every extreme that they name: `node_of`: at each section the nodes are runs of consecutive scenarios, numbered in order from 0; each node of a section lies within one node of the section before; section 0 is one node, the last section has 4 nodes, and node counts grow from section to section.
All inputs are finite; a program needn't handle non-finite values. No bound on the sum of `tile_mask` on one device may be relied on, other than what follows from the above.
Results may differ from a plain program's by a relative error of at most 0.0015.
Values may be sent and summed in bfloat16 or wider, within the bound.
A program may use at most 64 MiB of HBM per device.

v0:
```python
import jax
import jax.numpy as jnp
from jax import lax
from jax.sharding import PartitionSpec as P

ITERS = 8
RAMP_WEIGHT = 0.5
PENALTY = 1.0
STEP_PRIMAL = 0.3
STEP_INVEST = 0.5
STEP_DUAL = 0.3
STEP_CAP = 0.05


def with_halo(cells, sides, width):
    for axis, dim in sides:
        count = lax.axis_size(axis)
        ends = count - 1
        head = lax.slice_in_dim(cells, 0, width, axis=dim)
        tail = lax.slice_in_dim(cells, cells.shape[dim] - width, cells.shape[dim], axis=dim)
        cells = jnp.concatenate(
            [
                lax.ppermute(tail, axis, [(i, (i + 1) % count) for i in range(ends)]),
                cells,
                lax.ppermute(head, axis, [((i + 1) % count, i) for i in range(ends)]),
            ],
            axis=dim,
        )
    return cells


def safe_average(node_sum, node_mass):
    safe_mass = node_mass + (node_mass <= 0.0).astype(jnp.float32)
    return node_sum / safe_mass[:, :, None]


def shards(
    cost_rate,
    invest_cost,
    tile,
    tile_mask,
    demand,
    dispatch,
    dual,
    cap_dual,
    capacity,
    multiplier,
    consensus,
    scen_weight,
    node_of,
):
    matrix = tile[0] * tile_mask[0].astype(jnp.bfloat16)
    hours_all = dispatch.shape[1] * lax.axis_size("hour")
    reg_count = lax.axis_size("reg")
    reg_place = lax.axis_index("reg")
    cons_part = dual.shape[2] // reg_count
    first_row = reg_place * cons_part
    primal = dispatch
    cap_var = cap_dual
    invest = capacity
    dual_low = dual.astype(jnp.bfloat16)
    dual_var = dual
    for step_index in range(ITERS):
        padded = with_halo(primal, (("hour", 1),), 1)
        rough = 2.0 * primal - padded[:, :-2] - padded[:, 2:]
        pulled = jnp.einsum("shr,rc->shc", dual_low, matrix, preferred_element_type=jnp.float32)
        grad_x = cost_rate + RAMP_WEIGHT * rough - pulled + cap_var
        zmean = lax.psum(jnp.sum(cap_var, axis=1), "hour") / hours_all
        grad_u = invest_cost[None] + multiplier + PENALTY * (invest - consensus) - zmean[:, None, :]
        primal_new = jnp.maximum(primal - STEP_PRIMAL * grad_x, 0.0)
        invest_new = jnp.maximum(invest - STEP_INVEST * grad_u, 0.0)
        primal_ext = 2.0 * primal_new - primal
        invest_ext = 2.0 * invest_new - invest
        partial_rows = jnp.einsum(
            "shc,rc->shr",
            primal_ext.astype(jnp.bfloat16),
            matrix,
            preferred_element_type=jnp.float32,
        )
        image = lax.psum(partial_rows, "reg")
        dual_var = jnp.maximum(dual_var + STEP_DUAL * (demand - image), 0.0)
        dual_low = dual_var.astype(jnp.bfloat16)
        cap_var = jnp.maximum(
            cap_var + STEP_CAP * (primal_ext - jnp.sum(invest_ext, axis=1)[:, None, :]), 0.0
        )
        primal = primal_new
        invest = invest_new
    dual_out = lax.dynamic_slice_in_dim(dual_var, first_row, cons_part, 2)
    node_count = node_of.shape[1] * lax.axis_size("scen") // 2
    node_ids = jnp.arange(node_count, dtype=jnp.int32)
    one_hot = (node_of[:, :, None] == node_ids[None, None, :]).astype(jnp.float32)
    weighted = scen_weight[:, None, None] * invest
    node_sum = jnp.einsum("gsn,sgc->gnc", one_hot, weighted, precision=lax.Precision.HIGHEST)
    node_mass = jnp.einsum("gsn,s->gn", one_hot, scen_weight, precision=lax.Precision.HIGHEST)
    sum_total, mass_total = lax.psum((node_sum, node_mass), "scen")
    average = safe_average(sum_total, mass_total)
    spread_back = jnp.einsum("gsn,gnc->sgc", one_hot, average, precision=lax.Precision.HIGHEST)
    multiplier_out = multiplier + PENALTY * (invest - spread_back)
    return (primal, dual_out, invest, multiplier_out)


def solution(mesh):
    placed = (
        P("scen", "hour", "reg"),
        P(None, "reg"),
        P("hour", None, "reg"),
        P("hour", None, "reg"),
        P("scen", "hour", None),
        P("scen", "hour", "reg"),
        P("scen", "hour", None),
        P("scen", "hour", "reg"),
        P("scen", None, "reg"),
        P("scen", None, "reg"),
        P("scen", None, "reg"),
        P("scen"),
        P(None, "scen"),
    )
    return jax.shard_map(
        shards,
        mesh=mesh,
        in_specs=placed,
        out_specs=(
            P("scen", "hour", "reg"),
            P("scen", "hour", "reg"),
            P("scen", None, "reg"),
            P("scen", None, "reg"),
        ),
        check_vma=False,
    )
```

profile of v0, /device:TPU:1, one launch (start us, length us, event | category | flops | bytes accessed | tf_op | source)
XLA Modules:
  0.0 458.1 jit_solution(8639232075780562060)
XLA Ops:
  7.3 1.0 fusion.177
  8.3 4.0 collective-permute-start
  12.4 1.3 collective-permute-start.1
  13.7 1.5 reduce_sum.135
  15.1 36.1 %psum.127 = f32[4,512]{1,0:T(4,128)S(1)} all-reduce(f32[4,512]{1,0:T(4,128)S(1)} %reduce_sum.135), channel_id=1, replica_groups=mesh['scen'=2,'hour'=16,'reg'=4] {'hour'}, use_global_device_ids=true, to_apply=%region_2.0 | all-reduce | flops 2048 | bytes 16384 | tf_op jit(solution)/shard_map/psum | solution.py:68
  51.3 1.1 convert_multiply_fusion
  52.5 5.1 %fusion.169 = (f32[4,512]{1,0:T(4,128)S(1)}, f32[4,168,512]{2,1,0:T(8,128)}, f32[4,168,512]{2,1,0:T(8,128)S(1)}) fusion(f32[4,168,512]{2,1,0:T(8,128)} %param.20, f32[4,512]{1,0:T(4,128)S(1)} %get-tuple-element.22, f32[4,168,512]{2,1,0:T(8,128)} %param.18, f32[4,168,256]{2,1,0:T(8,128)S(1)} %copy-done.20, ...), kind=kOutput, calls=%fused_computation.223 | convolution fusion | flops 182867968 | bytes 7864320 | tf_op jit(solution)/shard_map/shr,rc->shc/dot_general | solution.py:66
  57.6 1.1 copy-done.11
  58.7 1.3 fusion.87
  60.1 0.9 fusion.176
  61.0 1.3 collective-permute-start.2
  62.3 1.3 collective-permute-start.3
  63.6 31.5 %psum.129 = f32[4,512]{1,0:T(4,128)S(1)} all-reduce(f32[4,512]{1,0:T(4,128)S(1)} %get-tuple-element.20), channel_id=1, replica_groups=mesh['scen'=2,'hour'=16,'reg'=4] {'hour'}, use_global_device_ids=true, to_apply=%region_6.0 | all-reduce | flops 2048 | bytes 16384 | tf_op jit(solution)/shard_map/psum | solution.py:68
  95.1 8.0 %all-reduce.10.cloned.1.call-done = f32[4,168,256]{2,1,0:T(8,128)} async-done(((f32[4,168,256]{2,1,0:T(8,128)}), f32[4,168,256]{2,1,0:T(8,128)}) %all-reduce.10.cloned.1.call-update) | async-done | bytes 688144 | tf_op jit(solution)/shard_map/psum | solution.py:80
  103.2 5.2 %fusion.168 = (f32[4,512]{1,0:T(4,128)S(1)}, f32[4,168,512]{2,1,0:T(8,128)}, f32[4,168,512]{2,1,0:T(8,128)S(1)}) fusion(f32[4,168,512]{2,1,0:T(8,128)} %get-tuple-element.21, f32[4,512]{1,0:T(4,128)S(1)} %subtract_reduce_fusion.5, f32[4,168,512]{2,1,0:T(8,128)} %copy-done.11, bf16[1,256,512]{2,1,0:T(8,128)(2,1)S(1)} %convert_multiply_fusion, ...), kind=kOutput, calls=%fused_computation.222 | convolution fusion | flops 183556096 | bytes 9240576 | tf_op jit(solution)/shard_map/shr,rc->shc/dot_general | solution.py:66
  108.4 1.1 copy-done.5
  109.5 1.3 fusion.85
  111.7 3.1 collective-permute-start.4
  114.8 1.3 collective-permute-start.5
  116.1 35.6 %psum.131 = f32[4,512]{1,0:T(4,128)S(1)} all-reduce(f32[4,512]{1,0:T(4,128)S(1)} %get-tuple-element.18), channel_id=1, replica_groups=mesh['scen'=2,'hour'=16,'reg'=4] {'hour'}, use_global_device_ids=true, to_apply=%region_10.0 | all-reduce | flops 2048 | bytes 16384 | tf_op jit(solution)/shard_map/psum | solution.py:68
  151.8 1.6 all-reduce.12.cloned.1.call-done
  153.4 1.9 add_maximum_fusion.12
  155.8 2.2 fusion.167
  158.0 1.1 copy-done.7
  159.1 1.3 fusion.83
  161.3 3.1 collective-permute-start.6
  164.4 1.3 collective-permute-start.7
  165.7 36.0 %psum.133 = f32[4,512]{1,0:T(4,128)S(1)} all-reduce(f32[4,512]{1,0:T(4,128)S(1)} %get-tuple-element.16), channel_id=1, replica_groups=mesh['scen'=2,'hour'=16,'reg'=4] {'hour'}, use_global_device_ids=true, to_apply=%region_14.0 | all-reduce | flops 2048 | bytes 16384 | tf_op jit(solution)/shard_map/psum | solution.py:68
  201.8 1.1 all-reduce.14.cloned.1.call-done
  202.9 5.2 %fusion.166 = (f32[4,512]{1,0:T(4,128)S(1)}, f32[4,168,512]{2,1,0:T(8,128)}, f32[4,168,512]{2,1,0:T(8,128)S(1)}) fusion(f32[4,168,512]{2,1,0:T(8,128)} %get-tuple-element.17, f32[4,512]{1,0:T(4,128)S(1)} %subtract_reduce_fusion.3, f32[4,168,512]{2,1,0:T(8,128)} %copy-done.7, bf16[1,256,512]{2,1,0:T(8,128)(2,1)S(1)} %convert_multiply_fusion, ...), kind=kOutput, calls=%fused_computation.220 | convolution fusion | flops 183556096 | bytes 9240576 | tf_op jit(solution)/shard_map/shr,rc->shc/dot_general | solution.py:66
  208.2 1.1 copy-done.3
  209.2 1.3 fusion.81
  211.5 3.1 collective-permute-start.8
  214.5 1.3 collective-permute-start.9
  215.8 35.3 %psum.135 = f32[4,512]{1,0:T(4,128)S(1)} all-reduce(f32[4,512]{1,0:T(4,128)S(1)} %get-tuple-element.14), channel_id=1, replica_groups=mesh['scen'=2,'hour'=16,'reg'=4] {'hour'}, use_global_device_ids=true, to_apply=%region_18.0 | all-reduce | flops 2048 | bytes 16384 | tf_op jit(solution)/shard_map/psum | solution.py:68
  251.3 1.9 all-reduce.16.cloned.1.call-done
  253.2 1.6 add_maximum_fusion.10
  255.3 2.2 fusion.165
  257.5 1.1 copy-done.9
  258.6 1.3 fusion.79
  260.9 3.1 collective-permute-start.10
  263.9 1.3 collective-permute-start.11
  265.2 35.5 %psum.137 = f32[4,512]{1,0:T(4,128)S(1)} all-reduce(f32[4,512]{1,0:T(4,128)S(1)} %get-tuple-element.12), channel_id=1, replica_groups=mesh['scen'=2,'hour'=16,'reg'=4] {'hour'}, use_global_device_ids=true, to_apply=%region_22.0 | all-reduce | flops 2048 | bytes 16384 | tf_op jit(solution)/shard_map/psum | solution.py:68
  300.9 1.9 all-reduce.18.cloned.1.call-done
  302.8 5.5 %fusion.164 = (f32[4,512]{1,0:T(4,128)S(1)}, f32[4,168,512]{2,1,0:T(8,128)}, f32[4,168,512]{2,1,0:T(8,128)S(1)}) fusion(f32[4,168,512]{2,1,0:T(8,128)} %get-tuple-element.13, f32[4,512]{1,0:T(4,128)S(1)} %subtract_reduce_fusion.1, f32[4,168,512]{2,1,0:T(8,128)} %copy-done.9, bf16[1,256,512]{2,1,0:T(8,128)(2,1)S(1)} %convert_multiply_fusion, ...), kind=kOutput, calls=%fused_computation.218 | convolution fusion | flops 183556096 | bytes 9240576 | tf_op jit(solution)/shard_map/shr,rc->shc/dot_general | solution.py:66
  308.3 1.3 fusion.77
  309.7 3.1 collective-permute-start.12
  312.8 1.3 collective-permute-start.13
  314.1 35.3 %psum.139 = f32[4,512]{1,0:T(4,128)S(1)} all-reduce(f32[4,512]{1,0:T(4,128)S(1)} %get-tuple-element.10), channel_id=1, replica_groups=mesh['scen'=2,'hour'=16,'reg'=4] {'hour'}, use_global_device_ids=true, to_apply=%region_26.0 | all-reduce | flops 2048 | bytes 16384 | tf_op jit(solution)/shard_map/psum | solution.py:68
  349.6 2.7 all-reduce.20.cloned.1.call-done
  352.3 3.4 fusion.139
  355.7 1.1 copy-done.13
  356.8 1.3 fusion.75
  358.4 0.9 fusion.170
  359.2 3.2 collective-permute-start.14
  362.5 1.3 collective-permute-start.15
  363.8 35.2 %psum.141 = f32[4,512]{1,0:T(4,128)S(1)} all-reduce(f32[4,512]{1,0:T(4,128)S(1)} %get-tuple-element.46), channel_id=1, replica_groups=mesh['scen'=2,'hour'=16,'reg'=4] {'hour'}, use_global_device_ids=true, to_apply=%region_30.0 | all-reduce | flops 2048 | bytes 16384 | tf_op jit(solution)/shard_map/psum | solution.py:68
  400.0 1.9 add_maximum_fusion.7
  402.7 1.0 fusion.7
  403.8 1.1 copy-done.18
  404.8 1.3 fusion.74
  406.4 9.4 %all-reduce = (f32[3,4,512]{2,1,0:T(4,128)S(1)}, f32[3,4]{1,0:T(4,128)S(1)}) all-reduce(f32[3,4,512]{2,1,0:T(4,128)S(1)} %fusion.140, f32[3,4]{1,0:T(4,128)S(1)} %bitcast.64), channel_id=1, replica_groups=mesh['scen'=2,'hour'=16,'reg'=4] {'scen'}, use_global_device_ids=true, to_apply=%region_31.0 | all-reduce | flops 6156 | bytes 49248 | tf_op jit(solution)/shard_map/psum | solution.py:95
  416.7 32.3 %all-reduce.24.cloned.1.call-done = f32[4,168,256]{2,1,0:T(8,128)} async-done(((f32[4,168,256]{2,1,0:T(8,128)}), f32[4,168,256]{2,1,0:T(8,128)}) %all-reduce.24.cloned.1.call-update) | async-done | bytes 688144 | tf_op jit(solution)/shard_map/psum | solution.py:80
  449.0 1.4 fusion.90
  (117 shorter events, 9.7 us)
Async XLA Ops:
  7.2 44.1 %copy-start.26 = (bf16[1,256,512]{2,1,0:T(8,128)(2,1)S(1)}, bf16[1,256,512]{2,1,0:T(8,128)(2,1)}, u32[]{:S(2)}) copy-start(bf16[1,256,512]{2,1,0:T(8,128)(2,1)} %param.15) | copy-start | bytes 786436
  7.2 45.2 %copy-start.29 = (f32[3,512]{1,0:T(4,128)S(1)}, f32[3,512]{1,0:T(4,128)}, u32[]{:S(2)}) copy-start(f32[3,512]{1,0:T(4,128)} %param.14) | copy-start | bytes 18436
  7.2 45.2 %copy-start.21 = (f32[4,3,512]{2,0,1:T(4,128)S(1)}, f32[4,3,512]{2,0,1:T(4,128)}, u32[]{:S(2)}) copy-start(f32[4,3,512]{2,0,1:T(4,128)} %param.21) | copy-start | bytes 73732
  7.2 45.2 %copy-start.28 = (f32[4,3,512]{2,0,1:T(4,128)S(1)}, f32[4,3,512]{2,0,1:T(4,128)}, u32[]{:S(2)}) copy-start(f32[4,3,512]{2,0,1:T(4,128)} %param.22) | copy-start | bytes 73732
  7.2 45.2 %copy-start.22 = (f32[4,3,512]{2,0,1:T(4,128)S(1)}, f32[4,3,512]{2,0,1:T(4,128)}, u32[]{:S(2)}) copy-start(f32[4,3,512]{2,0,1:T(4,128)} %param.23) | copy-start | bytes 73732
  7.2 45.2 %copy-start.1 = (f32[4,168,512]{2,1,0:T(8,128)S(1)}, f32[4,168,512]{2,1,0:T(8,128)}, u32[]{:S(2)}) copy-start(f32[4,168,512]{2,1,0:T(8,128)} %param.13) | copy-start | bytes 4128772
  7.2 45.2 %copy-start.20 = (f32[4,168,256]{2,1,0:T(8,128)S(1)}, f32[4,168,256]{2,1,0:T(8,128)}, u32[]{:S(2)}) copy-start(f32[4,168,256]{2,1,0:T(8,128)} %param.19) | copy-start | bytes 2064388
  7.2 95.9 %all-reduce.10.cloned.1.call-start = ((), (), s32[]{:S(2)}) async-start(), calls=%async_computation | async-start | bytes 1376256 | tf_op jit(solution)/shard_map/psum | solution.py:80
  8.3 44.1 %collective-permute-start = (f32[4,1,512]{2,1,0:T(1,128)S(1)}, f32[4,1,512]{2,1,0:T(1,128)S(1)}, u32[]{:S(2)}, u32[]{:S(2)}) collective-permute-start(f32[4,1,512]{2,1,0:T(1,128)S(1)} %get-tuple-element.38), channel_id=1, source_target_pairs={{0,4},{4,8},{8,12},{12,16},{16,20},{20,24},{24,28},{28,32},{32,36}... | collective-permute-start | bytes 24584 | tf_op jit(solution)/shard_map/ppermute | solution.py:23
  12.4 40.1 %collective-permute-start.1 = (f32[4,1,512]{2,1,0:T(1,128)S(1)}, f32[4,1,512]{2,1,0:T(1,128)S(1)}, u32[]{:S(2)}, u32[]{:S(2)}) collective-permute-start(f32[4,1,512]{2,1,0:T(1,128)S(1)} %get-tuple-element.39), channel_id=1, source_target_pairs={{4,0},{8,4},{12,8},{16,12},{20,16},{24,20},{28,24},{32,28},{36,32}... | collective-permute-start | bytes 24584 | tf_op jit(solution)/shard_map/ppermute | solution.py:25
  52.5 6.3 %copy-start.23 = (f32[4,168,512]{2,1,0:T(8,128)S(1)}, f32[4,168,512]{2,1,0:T(8,128)}, u32[]{:S(2)}) copy-start(f32[4,168,512]{2,1,0:T(8,128)} %param.18) | copy-start | bytes 4128772
  57.6 1.1 copy-start.11
  58.7 44.4 %copy-start = (f32[4,168,256]{2,1,0:T(8,128)S(1)}, f32[4,168,256]{2,1,0:T(8,128)}, u32[]{:S(2)}) copy-start(f32[4,168,256]{2,1,0:T(8,128)} %param.17) | copy-start | bytes 2064388
  60.0 93.4 %all-reduce.12.cloned.1.call-start = ((), (), s32[]{:S(2)}) async-start(), calls=%async_computation.1 | async-start | bytes 1376256 | tf_op jit(solution)/shard_map/psum | solution.py:80
  61.0 34.1 %collective-permute-start.2 = (f32[4,1,512]{2,1,0:T(1,128)S(1)}, f32[4,1,512]{2,1,0:T(1,128)S(1)}, u32[]{:S(2)}, u32[]{:S(2)}) collective-permute-start(f32[4,1,512]{2,1,0:T(1,128)S(1)} %get-tuple-element.36), channel_id=1, source_target_pairs={{0,4},{4,8},{8,12},{12,16},{16,20},{20,24},{24,28},{28,32},{32,36}... | collective-permute-start | bytes 24584 | tf_op jit(solution)/shard_map/ppermute | solution.py:23
  62.3 32.8 %collective-permute-start.3 = (f32[4,1,512]{2,1,0:T(1,128)S(1)}, f32[4,1,512]{2,1,0:T(1,128)S(1)}, u32[]{:S(2)}, u32[]{:S(2)}) collective-permute-start(f32[4,1,512]{2,1,0:T(1,128)S(1)} %get-tuple-element.37), channel_id=1, source_target_pairs={{4,0},{8,4},{12,8},{16,12},{20,16},{24,20},{28,24},{32,28},{36,32}... | collective-permute-start | bytes 24584 | tf_op jit(solution)/shard_map/ppermute | solution.py:25
  103.2 6.3 %copy-start.12 = (f32[4,168,512]{2,1,0:T(8,128)S(1)}, f32[4,168,512]{2,1,0:T(8,128)}, u32[]{:S(2)}) copy-start(f32[4,168,512]{2,1,0:T(8,128)} %copy-done.11) | copy-start | bytes 4128772
  108.4 1.1 copy-start.5
  110.8 92.1 %all-reduce.14.cloned.1.call-start = ((), (), s32[]{:S(2)}) async-start(), calls=%async_computation.2 | async-start | bytes 1376256 | tf_op jit(solution)/shard_map/psum | solution.py:80
  111.7 43.5 %collective-permute-start.4 = (f32[4,1,512]{2,1,0:T(1,128)S(1)}, f32[4,1,512]{2,1,0:T(1,128)S(1)}, u32[]{:S(2)}, u32[]{:S(2)}) collective-permute-start(f32[4,1,512]{2,1,0:T(1,128)S(1)} %get-tuple-element.34), channel_id=1, source_target_pairs={{0,4},{4,8},{8,12},{12,16},{16,20},{20,24},{24,28},{28,32},{32,36}... | collective-permute-start | bytes 24584 | tf_op jit(solution)/shard_map/ppermute | solution.py:23
  114.8 40.5 %collective-permute-start.5 = (f32[4,1,512]{2,1,0:T(1,128)S(1)}, f32[4,1,512]{2,1,0:T(1,128)S(1)}, u32[]{:S(2)}, u32[]{:S(2)}) collective-permute-start(f32[4,1,512]{2,1,0:T(1,128)S(1)} %get-tuple-element.35), channel_id=1, source_target_pairs={{4,0},{8,4},{12,8},{16,12},{20,16},{24,20},{28,24},{32,28},{36,32}... | collective-permute-start | bytes 24584 | tf_op jit(solution)/shard_map/ppermute | solution.py:25
  153.4 2.0 copy-start.6
  153.4 2.4 copy-start.25
  158.0 1.1 copy-start.7
  160.4 92.8 %all-reduce.16.cloned.1.call-start = ((), (), s32[]{:S(2)}) async-start(), calls=%async_computation.3 | async-start | bytes 1376256 | tf_op jit(solution)/shard_map/psum | solution.py:80
  161.3 40.5 %collective-permute-start.6 = (f32[4,1,512]{2,1,0:T(1,128)S(1)}, f32[4,1,512]{2,1,0:T(1,128)S(1)}, u32[]{:S(2)}, u32[]{:S(2)}) collective-permute-start(f32[4,1,512]{2,1,0:T(1,128)S(1)} %get-tuple-element.32), channel_id=1, source_target_pairs={{0,4},{4,8},{8,12},{12,16},{16,20},{20,24},{24,28},{28,32},{32,36}... | collective-permute-start | bytes 24584 | tf_op jit(solution)/shard_map/ppermute | solution.py:23
  164.4 37.4 %collective-permute-start.7 = (f32[4,1,512]{2,1,0:T(1,128)S(1)}, f32[4,1,512]{2,1,0:T(1,128)S(1)}, u32[]{:S(2)}, u32[]{:S(2)}) collective-permute-start(f32[4,1,512]{2,1,0:T(1,128)S(1)} %get-tuple-element.33), channel_id=1, source_target_pairs={{4,0},{8,4},{12,8},{16,12},{20,16},{24,20},{28,24},{32,28},{36,32}... | collective-permute-start | bytes 24584 | tf_op jit(solution)/shard_map/ppermute | solution.py:25
  202.9 6.3 %copy-start.8 = (f32[4,168,512]{2,1,0:T(8,128)S(1)}, f32[4,168,512]{2,1,0:T(8,128)}, u32[]{:S(2)}) copy-start(f32[4,168,512]{2,1,0:T(8,128)} %copy-done.7) | copy-start | bytes 4128772
  208.2 1.1 copy-start.3
  210.5 92.2 %all-reduce.18.cloned.1.call-start = ((), (), s32[]{:S(2)}) async-start(), calls=%async_computation.4 | async-start | bytes 1376256 | tf_op jit(solution)/shard_map/psum | solution.py:80
  211.5 43.4 %collective-permute-start.8 = (f32[4,1,512]{2,1,0:T(1,128)S(1)}, f32[4,1,512]{2,1,0:T(1,128)S(1)}, u32[]{:S(2)}, u32[]{:S(2)}) collective-permute-start(f32[4,1,512]{2,1,0:T(1,128)S(1)} %get-tuple-element.30), channel_id=1, source_target_pairs={{0,4},{4,8},{8,12},{12,16},{16,20},{20,24},{24,28},{28,32},{32,36}... | collective-permute-start | bytes 24584 | tf_op jit(solution)/shard_map/ppermute | solution.py:23
  214.5 40.3 %collective-permute-start.9 = (f32[4,1,512]{2,1,0:T(1,128)S(1)}, f32[4,1,512]{2,1,0:T(1,128)S(1)}, u32[]{:S(2)}, u32[]{:S(2)}) collective-permute-start(f32[4,1,512]{2,1,0:T(1,128)S(1)} %get-tuple-element.31), channel_id=1, source_target_pairs={{4,0},{8,4},{12,8},{16,12},{20,16},{24,20},{28,24},{32,28},{36,32}... | collective-permute-start | bytes 24584 | tf_op jit(solution)/shard_map/ppermute | solution.py:25
  253.2 1.8 copy-start.4
  253.2 2.2 copy-start.24
  254.8 2.7 copy-start.15
  257.5 1.1 copy-start.9
  258.6 44.1 %copy-start.16 = (f32[4,168,256]{2,1,0:T(8,128)S(1)}, f32[4,168,256]{2,1,0:T(8,128)}, u32[]{:S(2)}) copy-start(f32[4,168,256]{2,1,0:T(8,128)} %copy-done.15) | copy-start | bytes 2064388
  259.9 92.4 %all-reduce.20.cloned.1.call-start = ((), (), s32[]{:S(2)}) async-start(), calls=%async_computation.5 | async-start | bytes 1376256 | tf_op jit(solution)/shard_map/psum | solution.py:80
  260.9 40.0 %collective-permute-start.10 = (f32[4,1,512]{2,1,0:T(1,128)S(1)}, f32[4,1,512]{2,1,0:T(1,128)S(1)}, u32[]{:S(2)}, u32[]{:S(2)}) collective-permute-start(f32[4,1,512]{2,1,0:T(1,128)S(1)} %get-tuple-element.28), channel_id=1, source_target_pairs={{0,4},{4,8},{8,12},{12,16},{16,20},{20,24},{24,28},{28,32},{32,36}... | collective-permute-start | bytes 24584 | tf_op jit(solution)/shard_map/ppermute | solution.py:23
  263.9 36.9 %collective-permute-start.11 = (f32[4,1,512]{2,1,0:T(1,128)S(1)}, f32[4,1,512]{2,1,0:T(1,128)S(1)}, u32[]{:S(2)}, u32[]{:S(2)}) collective-permute-start(f32[4,1,512]{2,1,0:T(1,128)S(1)} %get-tuple-element.29), channel_id=1, source_target_pairs={{4,0},{8,4},{12,8},{16,12},{20,16},{24,20},{28,24},{32,28},{36,32}... | collective-permute-start | bytes 24584 | tf_op jit(solution)/shard_map/ppermute | solution.py:25
  302.8 5.5 %copy-start.10 = (f32[4,168,512]{2,1,0:T(8,128)S(1)}, f32[4,168,512]{2,1,0:T(8,128)}, u32[]{:S(2)}) copy-start(f32[4,168,512]{2,1,0:T(8,128)} %copy-done.9) | copy-start | bytes 4128772
  309.6 90.3 %all-reduce.22.cloned.1.call-start = ((), (), s32[]{:S(2)}) async-start(), calls=%async_computation.6 | async-start | bytes 1376256 | tf_op jit(solution)/shard_map/psum | solution.py:80
  309.7 39.8 %collective-permute-start.12 = (f32[4,1,512]{2,1,0:T(1,128)S(1)}, f32[4,1,512]{2,1,0:T(1,128)S(1)}, u32[]{:S(2)}, u32[]{:S(2)}) collective-permute-start(f32[4,1,512]{2,1,0:T(1,128)S(1)} %get-tuple-element.26), channel_id=1, source_target_pairs={{0,4},{4,8},{8,12},{12,16},{16,20},{20,24},{24,28},{28,32},{32,36}... | collective-permute-start | bytes 24584 | tf_op jit(solution)/shard_map/ppermute | solution.py:23
  312.8 36.8 %collective-permute-start.13 = (f32[4,1,512]{2,1,0:T(1,128)S(1)}, f32[4,1,512]{2,1,0:T(1,128)S(1)}, u32[]{:S(2)}, u32[]{:S(2)}) collective-permute-start(f32[4,1,512]{2,1,0:T(1,128)S(1)} %get-tuple-element.27), channel_id=1, source_target_pairs={{4,0},{8,4},{12,8},{16,12},{20,16},{24,20},{28,24},{32,28},{36,32}... | collective-permute-start | bytes 24584 | tf_op jit(solution)/shard_map/ppermute | solution.py:25
  355.7 1.1 copy-start.13
  356.8 1.4 copy-start.30
  356.8 1.4 copy-start.31
  358.1 90.9 %all-reduce.24.cloned.1.call-start = ((), (), s32[]{:S(2)}) async-start(), calls=%async_computation.7 | async-start | bytes 1376256 | tf_op jit(solution)/shard_map/psum | solution.py:80
  359.2 42.7 %collective-permute-start.14 = (f32[4,1,512]{2,1,0:T(1,128)S(1)}, f32[4,1,512]{2,1,0:T(1,128)S(1)}, u32[]{:S(2)}, u32[]{:S(2)}) collective-permute-start(f32[4,1,512]{2,1,0:T(1,128)S(1)} %get-tuple-element.24), channel_id=1, source_target_pairs={{0,4},{4,8},{8,12},{12,16},{16,20},{20,24},{24,28},{28,32},{32,36}... | collective-permute-start | bytes 24584 | tf_op jit(solution)/shard_map/ppermute | solution.py:23
  362.5 39.4 %collective-permute-start.15 = (f32[4,1,512]{2,1,0:T(1,128)S(1)}, f32[4,1,512]{2,1,0:T(1,128)S(1)}, u32[]{:S(2)}, u32[]{:S(2)}) collective-permute-start(f32[4,1,512]{2,1,0:T(1,128)S(1)} %get-tuple-element.25), channel_id=1, source_target_pairs={{4,0},{8,4},{12,8},{16,12},{20,16},{24,20},{28,24},{32,28},{36,32}... | collective-permute-start | bytes 24584 | tf_op jit(solution)/shard_map/ppermute | solution.py:25
  399.1 16.7 %copy-start.27 = (f32[4,3,512]{2,0,1:T(4,128)}, f32[4,3,512]{2,0,1:T(4,128)S(1)}, u32[]{:S(2)}) copy-start(f32[4,3,512]{2,0,1:T(4,128)S(1)} %subtract_maximum_fusion) | copy-start | bytes 73732
  399.9 2.0 copy-start.2
  399.9 2.4 copy-start.14
  399.9 2.8 copy-start.17
  401.9 1.9 copy-start.19
  403.8 1.1 copy-start.18
Sparse Core Ops, SparseCore 0:
  60.2 42.9 all-reduce.9
  110.9 42.4 all-reduce.11
  160.5 42.3 all-reduce.13
  210.6 42.4 all-reduce.15
  260.0 42.6 all-reduce.17
  309.7 42.4 all-reduce.19
  358.2 41.6 all-reduce.21
  406.3 42.6 all-reduce.23
where the time goes:
time: 459 us; the launch traced here: 458 us
  blocking collectives  290 us (63%)
  waiting for transfers between devices  50.6 us (11%)
  matrix products  41.5 us (9%)
  starting transfers between devices  34.5 us (8%)
  local copies, waits for them, and re-layouts  16.7 us (4%)
  between operations  14.8 us (3%)
  other arithmetic  10.1 us (2%)
    psum x8, blocking collectives, shards(): zmean = lax.psum(jnp.sum(cap_var, axis=1), 'hour') / hours_all  281 us
    psum x8, waiting for transfers between devices, shards(): image = lax.psum(partial_rows, 'reg')  50.4 us
    dot_general x8, matrix products, shards(): jnp.einsum('shr,rc->shc', dual_low, matrix, preferred_element_type=jnp.fl...  30 us
    ppermute x8, starting transfers between devices, with_halo(): lax.ppermute(tail, axis, [(i, (i + 1) % count) for i in range(ends)])  23.9 us
    unnamed x65, local copies, waits for them, and re-layouts  10.4 us
    ppermute x8, starting transfers between devices, with_halo(): lax.ppermute(head, axis, [((i + 1) % count, i) for i in range(ends)])  10.3 us
    dot_general x8, matrix products, shards(): jnp.einsum('shc,rc->shr', primal_ext.astype(jnp.bfloat16), matrix, prefer...  10.2 us
    psum x1, blocking collectives, shards(): sum_total, mass_total = lax.psum((node_sum, node_mass), 'scen')  9.39 us
  transfers between devices with their start and end apart: 24, of which 8 were waited for; matrix products, arithmetic and copies ran while one was open for 3% of the time, Pallas kernels for 0%

commit v1 on v0

--- a/solution.py
+++ b/solution.py
@@ -77,7 +77,7 @@
             matrix,
             preferred_element_type=jnp.float32,
         )
-        image = lax.psum(partial_rows, "reg")
+        image = jnp.sum(lax.all_gather(partial_rows, "reg"), axis=0)
         dual_var = jnp.maximum(dual_var + STEP_DUAL * (demand - image), 0.0)
         dual_low = dual_var.astype(jnp.bfloat16)
         cap_var = jnp.maximum(

time: 459 us -> 485 us (1.057); the launches traced: 458 us -> 476 us
  other arithmetic: 10.1 us -> 30.7 us
  blocking collectives: 290 us -> 285 us
    all_gather x0 -> x8, waiting for transfers between devices: none -> 53.2 us  [shards(): image = jnp.sum(lax.all_gather(partial_rows, 'reg'), axis=0)]
    psum x8 -> x0, waiting for transfers between devices: 50.4 us -> none  [shards(): image = lax.psum(partial_rows, 'reg')]
    reduce_sum x0 -> x8, other arithmetic: none -> 21.7 us  [shards(): image = jnp.sum(lax.all_gather(partial_rows, 'reg'), axis=0)]
    psum x8, blocking collectives: 281 us -> 275 us  [shards(): zmean = lax.psum(jnp.sum(cap_var, axis=1), 'hour') / hours_all]
    unnamed x65 -> x69, local copies, waits for them, and re-layouts: 10.4 us -> 10.3 us
  transfers between devices with their start and end apart: 24 -> 24, of which waited for: 8 -> 7; matrix products, arithmetic and copies ran while one was open for 3% -> 7% of each run, Pallas kernels for 0% -> 0%
where the time goes in v1:
time: 485 us; the launch traced here: 476 us
  blocking collectives  285 us (59%)
  waiting for transfers between devices  53.3 us (11%)
  matrix products  41.3 us (9%)
  starting transfers between devices  34.7 us (7%)
  other arithmetic  30.7 us (6%)
  local copies, waits for them, and re-layouts  16.6 us (3%)
  between operations  14.8 us (3%)
    psum x8, blocking collectives, shards(): zmean = lax.psum(jnp.sum(cap_var, axis=1), 'hour') / hours_all  275 us
    all_gather x8, waiting for transfers between devices, shards(): image = jnp.sum(lax.all_gather(partial_rows, 'reg'), axis=0)  53.2 us
    dot_general x8, matrix products, shards(): jnp.einsum('shr,rc->shc', dual_low, matrix, preferred_element_type=jnp.fl...  29.8 us
    ppermute x8, starting transfers between devices, with_halo(): lax.ppermute(tail, axis, [(i, (i + 1) % count) for i in range(ends)])  24 us
    reduce_sum x8, other arithmetic, shards(): image = jnp.sum(lax.all_gather(partial_rows, 'reg'), axis=0)  21.7 us
    ppermute x8, starting transfers between devices, with_halo(): lax.ppermute(head, axis, [((i + 1) % count, i) for i in range(ends)])  10.3 us
    unnamed x69, local copies, waits for them, and re-layouts  10.3 us
    dot_general x8, matrix products, shards(): jnp.einsum('shc,rc->shr', primal_ext.astype(jnp.bfloat16), matrix, prefer...  10.2 us
  transfers between devices with their start and end apart: 24, of which 7 were waited for; matrix products, arithmetic and copies ran while one was open for 7% of the time, Pallas kernels for 0%

profile of v1, /device:TPU:1, one launch (start us, length us, event | category | flops | bytes accessed | tf_op | source)
XLA Modules:
  0.0 476.3 jit_solution(18385368294072431387)
XLA Ops:
  8.3 4.0 collective-permute-start
  12.4 1.3 collective-permute-start.1
  13.7 1.5 reduce_sum.208
  15.1 36.1 %psum.70 = f32[4,512]{1,0:T(4,128)S(1)} all-reduce(f32[4,512]{1,0:T(4,128)S(1)} %reduce_sum.208), channel_id=1, replica_groups=mesh['scen'=2,'hour'=16,'reg'=4] {'hour'}, use_global_device_ids=true, to_apply=%region_2.0 | all-reduce | flops 2048 | bytes 16384 | tf_op jit(solution)/shard_map/psum | solution.py:68
  51.3 1.1 convert_multiply_fusion
  52.5 4.9 %fusion.169 = (f32[4,512]{1,0:T(4,128)S(1)}, f32[4,168,512]{2,1,0:T(8,128)}, f32[4,168,512]{2,1,0:T(8,128)S(1)}) fusion(f32[4,168,512]{2,1,0:T(8,128)} %param.20, f32[4,512]{1,0:T(4,128)S(1)} %get-tuple-element.22, f32[4,168,512]{2,1,0:T(8,128)} %param.18, f32[4,168,256]{2,1,0:T(8,128)S(1)} %copy-done.22, ...), kind=kOutput, calls=%fused_computation.223 | convolution fusion | flops 182867968 | bytes 7864320 | tf_op jit(solution)/shard_map/shr,rc->shc/dot_general | solution.py:66
  57.4 1.1 copy-done.11
  58.5 1.3 fusion.87
  60.7 1.3 collective-permute-start.2
  62.0 1.3 collective-permute-start.3
  63.3 31.5 %psum.71 = f32[4,512]{1,0:T(4,128)S(1)} all-reduce(f32[4,512]{1,0:T(4,128)S(1)} %get-tuple-element.20), channel_id=1, replica_groups=mesh['scen'=2,'hour'=16,'reg'=4] {'hour'}, use_global_device_ids=true, to_apply=%region_6.0 | all-reduce | flops 2048 | bytes 16384 | tf_op jit(solution)/shard_map/psum | solution.py:68
  94.9 4.0 all-gather.17.cloned.1.call-done
  98.9 2.1 reduce_sum.207
  101.0 5.3 %fusion.168 = (f32[4,512]{1,0:T(4,128)S(1)}, f32[4,168,512]{2,1,0:T(8,128)}, f32[4,168,512]{2,1,0:T(8,128)S(1)}) fusion(f32[4,168,512]{2,1,0:T(8,128)} %get-tuple-element.21, f32[4,512]{1,0:T(4,128)S(1)} %subtract_reduce_fusion.5, f32[4,168,512]{2,1,0:T(8,128)} %copy-done.11, bf16[1,256,512]{2,1,0:T(8,128)(2,1)S(1)} %convert_multiply_fusion, ...), kind=kOutput, calls=%fused_computation.222 | convolution fusion | flops 183556096 | bytes 9240576 | tf_op jit(solution)/shard_map/shr,rc->shc/dot_general | solution.py:66
  106.3 1.1 copy-done.5
  107.4 1.3 fusion.85
  109.6 3.1 collective-permute-start.4
  112.7 1.3 collective-permute-start.5
  114.0 34.7 %psum.72 = f32[4,512]{1,0:T(4,128)S(1)} all-reduce(f32[4,512]{1,0:T(4,128)S(1)} %get-tuple-element.18), channel_id=1, replica_groups=mesh['scen'=2,'hour'=16,'reg'=4] {'hour'}, use_global_device_ids=true, to_apply=%region_10.0 | all-reduce | flops 2048 | bytes 16384 | tf_op jit(solution)/shard_map/psum | solution.py:68
  148.8 2.4 all-gather.19.cloned.1.call-done
  151.3 2.9 reduce_sum.210
  154.2 1.9 add_maximum_fusion.12
  156.5 2.2 fusion.167
  158.8 1.1 copy-done.7
  159.8 1.3 fusion.83
  162.1 3.1 collective-permute-start.6
  165.2 1.3 collective-permute-start.7
  166.5 34.7 %psum.73 = f32[4,512]{1,0:T(4,128)S(1)} all-reduce(f32[4,512]{1,0:T(4,128)S(1)} %get-tuple-element.16), channel_id=1, replica_groups=mesh['scen'=2,'hour'=16,'reg'=4] {'hour'}, use_global_device_ids=true, to_apply=%region_14.0 | all-reduce | flops 2048 | bytes 16384 | tf_op jit(solution)/shard_map/psum | solution.py:68
  201.3 2.4 all-gather.21.cloned.1.call-done
  203.7 2.9 reduce_sum.213
  206.7 5.2 %fusion.166 = (f32[4,512]{1,0:T(4,128)S(1)}, f32[4,168,512]{2,1,0:T(8,128)}, f32[4,168,512]{2,1,0:T(8,128)S(1)}) fusion(f32[4,168,512]{2,1,0:T(8,128)} %get-tuple-element.17, f32[4,512]{1,0:T(4,128)S(1)} %subtract_reduce_fusion.3, f32[4,168,512]{2,1,0:T(8,128)} %copy-done.7, bf16[1,256,512]{2,1,0:T(8,128)(2,1)S(1)} %convert_multiply_fusion, ...), kind=kOutput, calls=%fused_computation.220 | convolution fusion | flops 183556096 | bytes 9240576 | tf_op jit(solution)/shard_map/shr,rc->shc/dot_general | solution.py:66
  212.9 1.3 fusion.81
  215.2 3.1 collective-permute-start.8
  218.3 1.3 collective-permute-start.9
  219.6 34.7 %psum.74 = f32[4,512]{1,0:T(4,128)S(1)} all-reduce(f32[4,512]{1,0:T(4,128)S(1)} %get-tuple-element.14), channel_id=1, replica_groups=mesh['scen'=2,'hour'=16,'reg'=4] {'hour'}, use_global_device_ids=true, to_apply=%region_18.0 | all-reduce | flops 2048 | bytes 16384 | tf_op jit(solution)/shard_map/psum | solution.py:68
  254.4 2.4 all-gather.23.cloned.1.call-done
  256.9 2.9 reduce_sum.216
  259.8 1.6 add_maximum_fusion.10
  261.9 2.2 fusion.165
  264.1 1.1 copy-done.9
  265.2 1.3 fusion.79
  267.4 3.1 collective-permute-start.10
  270.6 1.3 collective-permute-start.11
  271.9 34.9 %psum.75 = f32[4,512]{1,0:T(4,128)S(1)} all-reduce(f32[4,512]{1,0:T(4,128)S(1)} %get-tuple-element.12), channel_id=1, replica_groups=mesh['scen'=2,'hour'=16,'reg'=4] {'hour'}, use_global_device_ids=true, to_apply=%region_22.0 | all-reduce | flops 2048 | bytes 16384 | tf_op jit(solution)/shard_map/psum | solution.py:68
  306.9 2.2 all-gather.25.cloned.1.call-done
  309.1 3.0 reduce_sum.219
  312.1 5.6 %fusion.164 = (f32[4,512]{1,0:T(4,128)S(1)}, f32[4,168,512]{2,1,0:T(8,128)}, f32[4,168,512]{2,1,0:T(8,128)S(1)}) fusion(f32[4,168,512]{2,1,0:T(8,128)} %get-tuple-element.13, f32[4,512]{1,0:T(4,128)S(1)} %subtract_reduce_fusion.1, f32[4,168,512]{2,1,0:T(8,128)} %copy-done.9, bf16[1,256,512]{2,1,0:T(8,128)(2,1)S(1)} %convert_multiply_fusion, ...), kind=kOutput, calls=%fused_computation.218 | convolution fusion | flops 183556096 | bytes 9240576 | tf_op jit(solution)/shard_map/shr,rc->shc/dot_general | solution.py:66
  317.7 1.3 fusion.77
  319.1 3.1 collective-permute-start.12
  322.2 1.3 collective-permute-start.13
  323.5 34.9 %psum.76 = f32[4,512]{1,0:T(4,128)S(1)} all-reduce(f32[4,512]{1,0:T(4,128)S(1)} %get-tuple-element.10), channel_id=1, replica_groups=mesh['scen'=2,'hour'=16,'reg'=4] {'hour'}, use_global_device_ids=true, to_apply=%region_26.0 | all-reduce | flops 2048 | bytes 16384 | tf_op jit(solution)/shard_map/psum | solution.py:68
  358.5 3.3 all-gather.27.cloned.1.call-done
  361.8 2.9 reduce_sum.222
  364.7 3.4 fusion.139
  369.2 1.3 fusion.75
  371.5 3.1 collective-permute-start.14
  374.6 1.3 collective-permute-start.15
  375.9 36.4 %all-gather.29.cloned.1.call-done = f32[16,168,256]{2,1,0:T(8,128)} async-done(((f32[4,168,256]{2,1,0:T(8,128)}), f32[16,168,256]{2,1,0:T(8,128)}) %all-gather.29.cloned.1.call-update) | async-done | bytes 2752528 | tf_op jit(solution)/shard_map/all_gather | solution.py:80
  412.3 2.9 reduce_sum.225
  415.3 1.9 add_maximum_fusion.7
  420.2 1.3 fusion.74
  421.7 33.8 %psum.77 = f32[4,512]{1,0:T(4,128)S(1)} all-reduce(f32[4,512]{1,0:T(4,128)S(1)} %get-tuple-element.46), channel_id=1, replica_groups=mesh['scen'=2,'hour'=16,'reg'=4] {'hour'}, use_global_device_ids=true, to_apply=%region_30.0 | all-reduce | flops 2048 | bytes 16384 | tf_op jit(solution)/shard_map/psum | solution.py:68
  455.9 9.3 %all-reduce = (f32[3,4,512]{2,1,0:T(4,128)S(1)}, f32[3,4]{1,0:T(4,128)S(1)}) all-reduce(f32[3,4,512]{2,1,0:T(4,128)S(1)} %fusion.140, f32[3,4]{1,0:T(4,128)S(1)} %bitcast.80), channel_id=1, replica_groups=mesh['scen'=2,'hour'=16,'reg'=4] {'scen'}, use_global_device_ids=true, to_apply=%region_31.0 | all-reduce | flops 6156 | bytes 49248 | tf_op jit(solution)/shard_map/psum | solution.py:95
  466.1 2.1 reduce_sum.228
  (129 shorter events, 16.2 us)
Async XLA Ops:
  7.2 44.1 %copy-start.28 = (bf16[1,256,512]{2,1,0:T(8,128)(2,1)S(1)}, bf16[1,256,512]{2,1,0:T(8,128)(2,1)}, u32[]{:S(2)}) copy-start(bf16[1,256,512]{2,1,0:T(8,128)(2,1)} %param.15) | copy-start | bytes 786436
  7.2 45.2 %copy-start.31 = (f32[3,512]{1,0:T(4,128)S(1)}, f32[3,512]{1,0:T(4,128)}, u32[]{:S(2)}) copy-start(f32[3,512]{1,0:T(4,128)} %param.14) | copy-start | bytes 18436
  7.2 45.2 %copy-start.23 = (f32[4,3,512]{2,0,1:T(4,128)S(1)}, f32[4,3,512]{2,0,1:T(4,128)}, u32[]{:S(2)}) copy-start(f32[4,3,512]{2,0,1:T(4,128)} %param.21) | copy-start | bytes 73732
  7.2 45.2 %copy-start.30 = (f32[4,3,512]{2,0,1:T(4,128)S(1)}, f32[4,3,512]{2,0,1:T(4,128)}, u32[]{:S(2)}) copy-start(f32[4,3,512]{2,0,1:T(4,128)} %param.22) | copy-start | bytes 73732
  7.2 45.2 %copy-start.24 = (f32[4,3,512]{2,0,1:T(4,128)S(1)}, f32[4,3,512]{2,0,1:T(4,128)}, u32[]{:S(2)}) copy-start(f32[4,3,512]{2,0,1:T(4,128)} %param.23) | copy-start | bytes 73732
  7.2 45.2 %copy-start.1 = (f32[4,168,512]{2,1,0:T(8,128)S(1)}, f32[4,168,512]{2,1,0:T(8,128)}, u32[]{:S(2)}) copy-start(f32[4,168,512]{2,1,0:T(8,128)} %param.13) | copy-start | bytes 4128772
  7.2 45.2 %copy-start.22 = (f32[4,168,256]{2,1,0:T(8,128)S(1)}, f32[4,168,256]{2,1,0:T(8,128)}, u32[]{:S(2)}) copy-start(f32[4,168,256]{2,1,0:T(8,128)} %param.19) | copy-start | bytes 2064388
  7.2 91.6 %all-gather.17.cloned.1.call-start = ((), (), s32[]{:S(2)}) async-start(), calls=%async_computation | async-start | bytes 3440640 | tf_op jit(solution)/shard_map/all_gather | solution.py:80
  8.3 44.1 %collective-permute-start = (f32[4,1,512]{2,1,0:T(1,128)S(1)}, f32[4,1,512]{2,1,0:T(1,128)S(1)}, u32[]{:S(2)}, u32[]{:S(2)}) collective-permute-start(f32[4,1,512]{2,1,0:T(1,128)S(1)} %get-tuple-element.38), channel_id=1, source_target_pairs={{0,4},{4,8},{8,12},{12,16},{16,20},{20,24},{24,28},{28,32},{32,36}... | collective-permute-start | bytes 24584 | tf_op jit(solution)/shard_map/ppermute | solution.py:23
  12.4 40.1 %collective-permute-start.1 = (f32[4,1,512]{2,1,0:T(1,128)S(1)}, f32[4,1,512]{2,1,0:T(1,128)S(1)}, u32[]{:S(2)}, u32[]{:S(2)}) collective-permute-start(f32[4,1,512]{2,1,0:T(1,128)S(1)} %get-tuple-element.39), channel_id=1, source_target_pairs={{4,0},{8,4},{12,8},{16,12},{20,16},{24,20},{28,24},{32,28},{36,32}... | collective-permute-start | bytes 24584 | tf_op jit(solution)/shard_map/ppermute | solution.py:25
  52.5 6.0 %copy-start.25 = (f32[4,168,512]{2,1,0:T(8,128)S(1)}, f32[4,168,512]{2,1,0:T(8,128)}, u32[]{:S(2)}) copy-start(f32[4,168,512]{2,1,0:T(8,128)} %param.18) | copy-start | bytes 4128772
  57.4 1.1 copy-start.11
  59.8 91.5 %all-gather.19.cloned.1.call-start = ((), (), s32[]{:S(2)}) async-start(), calls=%async_computation.1 | async-start | bytes 3440640 | tf_op jit(solution)/shard_map/all_gather | solution.py:80
  60.7 40.3 %collective-permute-start.2 = (f32[4,1,512]{2,1,0:T(1,128)S(1)}, f32[4,1,512]{2,1,0:T(1,128)S(1)}, u32[]{:S(2)}, u32[]{:S(2)}) collective-permute-start(f32[4,1,512]{2,1,0:T(1,128)S(1)} %get-tuple-element.36), channel_id=1, source_target_pairs={{0,4},{4,8},{8,12},{12,16},{16,20},{20,24},{24,28},{28,32},{32,36}... | collective-permute-start | bytes 24584 | tf_op jit(solution)/shard_map/ppermute | solution.py:23
  62.0 39.0 %collective-permute-start.3 = (f32[4,1,512]{2,1,0:T(1,128)S(1)}, f32[4,1,512]{2,1,0:T(1,128)S(1)}, u32[]{:S(2)}, u32[]{:S(2)}) collective-permute-start(f32[4,1,512]{2,1,0:T(1,128)S(1)} %get-tuple-element.37), channel_id=1, source_target_pairs={{4,0},{8,4},{12,8},{16,12},{20,16},{24,20},{28,24},{32,28},{36,32}... | collective-permute-start | bytes 24584 | tf_op jit(solution)/shard_map/ppermute | solution.py:25
  98.9 2.1 copy-start
  101.0 5.3 %copy-start.15 = (f32[4,168,256]{2,1,0:T(8,128)}, f32[4,168,256]{2,1,0:T(8,128)S(1)}, u32[]{:S(2)}) copy-start(f32[4,168,256]{2,1,0:T(8,128)S(1)} %reduce_sum.207) | copy-start | bytes 2064388
  101.0 6.3 %copy-start.12 = (f32[4,168,512]{2,1,0:T(8,128)S(1)}, f32[4,168,512]{2,1,0:T(8,128)}, u32[]{:S(2)}) copy-start(f32[4,168,512]{2,1,0:T(8,128)} %copy-done.11) | copy-start | bytes 4128772
  106.3 1.1 copy-start.5
  108.7 95.0 %all-gather.21.cloned.1.call-start = ((), (), s32[]{:S(2)}) async-start(), calls=%async_computation.2 | async-start | bytes 3440640 | tf_op jit(solution)/shard_map/all_gather | solution.py:80
  109.6 46.4 %collective-permute-start.4 = (f32[4,1,512]{2,1,0:T(1,128)S(1)}, f32[4,1,512]{2,1,0:T(1,128)S(1)}, u32[]{:S(2)}, u32[]{:S(2)}) collective-permute-start(f32[4,1,512]{2,1,0:T(1,128)S(1)} %get-tuple-element.34), channel_id=1, source_target_pairs={{0,4},{4,8},{8,12},{12,16},{16,20},{20,24},{24,28},{28,32},{32,36}... | collective-permute-start | bytes 24584 | tf_op jit(solution)/shard_map/ppermute | solution.py:23
  112.7 43.3 %collective-permute-start.5 = (f32[4,1,512]{2,1,0:T(1,128)S(1)}, f32[4,1,512]{2,1,0:T(1,128)S(1)}, u32[]{:S(2)}, u32[]{:S(2)}) collective-permute-start(f32[4,1,512]{2,1,0:T(1,128)S(1)} %get-tuple-element.35), channel_id=1, source_target_pairs={{4,0},{8,4},{12,8},{16,12},{20,16},{24,20},{28,24},{32,28},{36,32}... | collective-permute-start | bytes 24584 | tf_op jit(solution)/shard_map/ppermute | solution.py:25
  154.2 2.0 copy-start.6
  154.2 2.4 copy-start.27
  158.8 1.1 copy-start.7
  161.1 95.7 %all-gather.23.cloned.1.call-start = ((), (), s32[]{:S(2)}) async-start(), calls=%async_computation.3 | async-start | bytes 3440640 | tf_op jit(solution)/shard_map/all_gather | solution.py:80
  162.1 44.6 %collective-permute-start.6 = (f32[4,1,512]{2,1,0:T(1,128)S(1)}, f32[4,1,512]{2,1,0:T(1,128)S(1)}, u32[]{:S(2)}, u32[]{:S(2)}) collective-permute-start(f32[4,1,512]{2,1,0:T(1,128)S(1)} %get-tuple-element.32), channel_id=1, source_target_pairs={{0,4},{4,8},{8,12},{12,16},{16,20},{20,24},{24,28},{28,32},{32,36}... | collective-permute-start | bytes 24584 | tf_op jit(solution)/shard_map/ppermute | solution.py:23
  165.2 41.5 %collective-permute-start.7 = (f32[4,1,512]{2,1,0:T(1,128)S(1)}, f32[4,1,512]{2,1,0:T(1,128)S(1)}, u32[]{:S(2)}, u32[]{:S(2)}) collective-permute-start(f32[4,1,512]{2,1,0:T(1,128)S(1)} %get-tuple-element.33), channel_id=1, source_target_pairs={{4,0},{8,4},{12,8},{16,12},{20,16},{24,20},{28,24},{32,28},{36,32}... | collective-permute-start | bytes 24584 | tf_op jit(solution)/shard_map/ppermute | solution.py:25
  206.7 6.3 %copy-start.8 = (f32[4,168,512]{2,1,0:T(8,128)S(1)}, f32[4,168,512]{2,1,0:T(8,128)}, u32[]{:S(2)}) copy-start(f32[4,168,512]{2,1,0:T(8,128)} %copy-done.7) | copy-start | bytes 4128772
  211.9 1.1 copy-start.3
  214.2 94.9 %all-gather.25.cloned.1.call-start = ((), (), s32[]{:S(2)}) async-start(), calls=%async_computation.4 | async-start | bytes 3440640 | tf_op jit(solution)/shard_map/all_gather | solution.py:80
  215.2 46.2 %collective-permute-start.8 = (f32[4,1,512]{2,1,0:T(1,128)S(1)}, f32[4,1,512]{2,1,0:T(1,128)S(1)}, u32[]{:S(2)}, u32[]{:S(2)}) collective-permute-start(f32[4,1,512]{2,1,0:T(1,128)S(1)} %get-tuple-element.30), channel_id=1, source_target_pairs={{0,4},{4,8},{8,12},{12,16},{16,20},{20,24},{24,28},{28,32},{32,36}... | collective-permute-start | bytes 24584 | tf_op jit(solution)/shard_map/ppermute | solution.py:23
  218.3 43.1 %collective-permute-start.9 = (f32[4,1,512]{2,1,0:T(1,128)S(1)}, f32[4,1,512]{2,1,0:T(1,128)S(1)}, u32[]{:S(2)}, u32[]{:S(2)}) collective-permute-start(f32[4,1,512]{2,1,0:T(1,128)S(1)} %get-tuple-element.31), channel_id=1, source_target_pairs={{4,0},{8,4},{12,8},{16,12},{20,16},{24,20},{28,24},{32,28},{36,32}... | collective-permute-start | bytes 24584 | tf_op jit(solution)/shard_map/ppermute | solution.py:25
  259.8 1.8 copy-start.4
  259.8 2.2 copy-start.26
  261.4 2.7 copy-start.16
  264.1 1.1 copy-start.9
  266.5 95.3 %all-gather.27.cloned.1.call-start = ((), (), s32[]{:S(2)}) async-start(), calls=%async_computation.5 | async-start | bytes 3440640 | tf_op jit(solution)/shard_map/all_gather | solution.py:80
  267.4 44.7 %collective-permute-start.10 = (f32[4,1,512]{2,1,0:T(1,128)S(1)}, f32[4,1,512]{2,1,0:T(1,128)S(1)}, u32[]{:S(2)}, u32[]{:S(2)}) collective-permute-start(f32[4,1,512]{2,1,0:T(1,128)S(1)} %get-tuple-element.28), channel_id=1, source_target_pairs={{0,4},{4,8},{8,12},{12,16},{16,20},{20,24},{24,28},{28,32},{32,36}... | collective-permute-start | bytes 24584 | tf_op jit(solution)/shard_map/ppermute | solution.py:23
  270.6 41.5 %collective-permute-start.11 = (f32[4,1,512]{2,1,0:T(1,128)S(1)}, f32[4,1,512]{2,1,0:T(1,128)S(1)}, u32[]{:S(2)}, u32[]{:S(2)}) collective-permute-start(f32[4,1,512]{2,1,0:T(1,128)S(1)} %get-tuple-element.29), channel_id=1, source_target_pairs={{4,0},{8,4},{12,8},{16,12},{20,16},{24,20},{28,24},{32,28},{36,32}... | collective-permute-start | bytes 24584 | tf_op jit(solution)/shard_map/ppermute | solution.py:25
  309.1 3.0 copy-start.17
  312.1 5.6 %copy-start.10 = (f32[4,168,512]{2,1,0:T(8,128)S(1)}, f32[4,168,512]{2,1,0:T(8,128)}, u32[]{:S(2)}) copy-start(f32[4,168,512]{2,1,0:T(8,128)} %copy-done.9) | copy-start | bytes 4128772
  319.0 93.3 %all-gather.29.cloned.1.call-start = ((), (), s32[]{:S(2)}) async-start(), calls=%async_computation.6 | async-start | bytes 3440640 | tf_op jit(solution)/shard_map/all_gather | solution.py:80
  319.1 45.7 %collective-permute-start.12 = (f32[4,1,512]{2,1,0:T(1,128)S(1)}, f32[4,1,512]{2,1,0:T(1,128)S(1)}, u32[]{:S(2)}, u32[]{:S(2)}) collective-permute-start(f32[4,1,512]{2,1,0:T(1,128)S(1)} %get-tuple-element.26), channel_id=1, source_target_pairs={{0,4},{4,8},{8,12},{12,16},{16,20},{20,24},{24,28},{28,32},{32,36}... | collective-permute-start | bytes 24584 | tf_op jit(solution)/shard_map/ppermute | solution.py:23
  322.2 42.5 %collective-permute-start.13 = (f32[4,1,512]{2,1,0:T(1,128)S(1)}, f32[4,1,512]{2,1,0:T(1,128)S(1)}, u32[]{:S(2)}, u32[]{:S(2)}) collective-permute-start(f32[4,1,512]{2,1,0:T(1,128)S(1)} %get-tuple-element.27), channel_id=1, source_target_pairs={{4,0},{8,4},{12,8},{16,12},{20,16},{24,20},{28,24},{32,28},{36,32}... | collective-permute-start | bytes 24584 | tf_op jit(solution)/shard_map/ppermute | solution.py:25
  368.1 1.1 copy-start.13
  370.5 95.6 %all-gather.31.cloned.1.call-start = ((), (), s32[]{:S(2)}) async-start(), calls=%async_computation.7 | async-start | bytes 3440640 | tf_op jit(solution)/shard_map/all_gather | solution.py:80
  371.5 45.7 %collective-permute-start.14 = (f32[4,1,512]{2,1,0:T(1,128)S(1)}, f32[4,1,512]{2,1,0:T(1,128)S(1)}, u32[]{:S(2)}, u32[]{:S(2)}) collective-permute-start(f32[4,1,512]{2,1,0:T(1,128)S(1)} %get-tuple-element.24), channel_id=1, source_target_pairs={{0,4},{4,8},{8,12},{12,16},{16,20},{20,24},{24,28},{28,32},{32,36}... | collective-permute-start | bytes 24584 | tf_op jit(solution)/shard_map/ppermute | solution.py:23
  374.6 42.6 %collective-permute-start.15 = (f32[4,1,512]{2,1,0:T(1,128)S(1)}, f32[4,1,512]{2,1,0:T(1,128)S(1)}, u32[]{:S(2)}, u32[]{:S(2)}) collective-permute-start(f32[4,1,512]{2,1,0:T(1,128)S(1)} %get-tuple-element.25), channel_id=1, source_target_pairs={{4,0},{8,4},{12,8},{16,12},{20,16},{24,20},{28,24},{32,28},{36,32}... | collective-permute-start | bytes 24584 | tf_op jit(solution)/shard_map/ppermute | solution.py:25
  415.2 2.0 copy-start.2
  415.3 2.4 copy-start.14
  415.3 2.8 copy-start.18
  417.2 1.9 copy-start.20
  419.1 1.1 copy-start.19
  420.1 1.3 copy-start.32
  420.1 1.3 copy-start.33
  455.6 12.6 %copy-start.29 = (f32[4,3,512]{2,0,1:T(4,128)}, f32[4,3,512]{2,0,1:T(4,128)S(1)}, u32[]{:S(2)}) copy-start(f32[4,3,512]{2,0,1:T(4,128)S(1)} %subtract_maximum_fusion) | copy-start | bytes 73732
  466.1 2.1 copy-start.21
Sparse Core Ops, SparseCore 0:
  59.9 38.9 all-gather.16
  108.8 42.4 all-gather.18
  161.2 42.4 all-gather.20
  214.4 42.4 all-gather.22
  266.6 42.4 all-gather.24
  319.1 42.6 all-gather.26
  370.7 41.6 all-gather.28
  421.6 35.3 all-gather.30
